TPU v7x, 32 devices: a whole 2x2x4 slice. The times are simulated.
32 devices in a mesh: group: 8 (over z, y), row: 4 (over x, core).
Axes of the slice: x: 2, y: 2, z: 4, core: 2. Of those that a mesh axis runs over, the one named last changes fastest.
Arguments:
- frames: bfloat16 [48, 16, 32, 384], P('group', 'row'), may hold values from -30 to 30
- clip_lengths: int32 [3], replicated, may hold values from 2 to 11, as said below
- group_start: int32 [8], P('group'), may hold values from 0 to 22, as said below
- group_count: int32 [8], P('group'), may hold values from 2 to 6, as said below
- kernel_one: bfloat16 [3, 3, 3, 384, 384], P(None, None, None, 'group'), may hold values from -0.0625 to 0.0625
- kernel_two: bfloat16 [3, 3, 3, 384, 384], P(None, None, None, 'group'), may hold values from -0.0625 to 0.0625
- gain_one: float32 [384], replicated, may hold values from 0.1 to 1.9
- gain_two: float32 [384], replicated, may hold values from 0.1 to 1.9
Outputs:
- decoded: bfloat16 [48, 16, 32, 384], P('group', 'row')
Inputs may be any that keep to these rules, and one draw needn't show every extreme that they name: group_start is the exclusive prefix sum of group_count over the devices. `group_count`: a quarter of the devices, never the last one, hold 6 frames, the others 2; the counts sum to 24. `clip_lengths`: one clip has exactly 11 frames; the three sum to 24.
All inputs are finite; a program needn't handle non-finite values.
Results may differ from a plain program's by a relative error of at most 0.0029.
Values may be sent and summed in bfloat16 or wider, within the bound.
A program may use at most 128 MiB of HBM per device.

v0:
```python
import jax
import jax.numpy as jnp
from jax import lax
from jax.sharding import PartitionSpec as P


def passed_along(array, axis, by):
    length = lax.axis_size(axis)
    pairs = [(i, i + by) for i in range(length) if 0 <= i + by < length]
    return lax.ppermute(array, axis, pairs)


def with_halo(cells, sides, width):
    for axis, dim in sides:
        count = lax.axis_size(axis)
        ends = count - 1
        head = lax.slice_in_dim(cells, 0, width, axis=dim)
        tail = lax.slice_in_dim(cells, cells.shape[dim] - width, cells.shape[dim], axis=dim)
        cells = jnp.concatenate(
            [
                lax.ppermute(tail, axis, [(i, (i + 1) % count) for i in range(ends)]),
                cells,
                lax.ppermute(head, axis, [((i + 1) % count, i) for i in range(ends)]),
            ],
            axis=dim,
        )
    return cells


def clip_positions(clip_lengths, frame_index):
    ends = jnp.cumsum(clip_lengths)
    begins = jnp.max(jnp.where(ends[None, :] <= frame_index[:, None], ends[None, :], 0), axis=1)
    return frame_index - begins


def norm_act(values, gain):
    data = values.astype(jnp.float32)
    mean_square = jnp.mean(data * data, axis=-1, keepdims=True)
    scaled = data * lax.rsqrt(mean_square + 1e-06)
    return jax.nn.silu(scaled * gain).astype(jnp.bfloat16)


def spatial_taps(padded, kernel_piece, lag_weights):
    in_count = kernel_piece.shape[3]
    inputs = lax.slice_in_dim(padded, 0, in_count, axis=3)
    slot_count = padded.shape[0] - 2
    summed = None
    for lag_index in range(3):
        window = inputs[lag_index : lag_index + slot_count]
        contrib = lax.conv_general_dilated(
            window,
            kernel_piece[lag_index],
            (1, 1),
            ((0, 0), (1, 1)),
            dimension_numbers=("NHWC", "HWIO", "NHWC"),
            preferred_element_type=jnp.float32,
        )
        contrib = contrib * lag_weights[lag_index][:, None, None, None]
        summed = contrib if summed is None else summed + contrib
    return summed


def per_device(
    frames, clip_lengths, group_start, group_count, kernel_one, kernel_two, gain_one, gain_two
):
    slot_count = frames.shape[0]
    frame_index = group_start[0] + jnp.arange(slot_count, dtype=jnp.int32)
    position = clip_positions(clip_lengths, frame_index)
    lag_weights = (
        (position >= 2).astype(jnp.float32),
        (position >= 1).astype(jnp.float32),
        jnp.ones((slot_count,), jnp.float32),
    )
    live_frames = jnp.arange(slot_count, dtype=jnp.int32) < group_count[0]

    def extend(acts):
        last_two = lax.dynamic_slice_in_dim(acts, group_count[0] - 2, 2, 0)
        carried = passed_along(last_two, "group", 1)
        return with_halo(jnp.concatenate([carried, acts], 0), (("row", 1),), 1)

    first_padded = extend(norm_act(frames, gain_one))
    zero_sums = jnp.zeros(frames.shape, jnp.float32)
    first_conv = zero_sums + spatial_taps(
        first_padded, lax.all_gather(kernel_one, "group", axis=3, tiled=True), lag_weights
    )
    second_padded = extend(norm_act(first_conv, gain_two))
    second_conv = zero_sums + spatial_taps(
        second_padded, lax.all_gather(kernel_two, "group", axis=3, tiled=True), lag_weights
    )
    summed = frames.astype(jnp.float32) + second_conv
    return jnp.where(live_frames[:, None, None, None], summed, 0.0).astype(jnp.bfloat16)


def solution(mesh):
    return jax.shard_map(
        per_device,
        mesh=mesh,
        in_specs=(
            P("group", "row", None, None),
            P(),
            P("group"),
            P("group"),
            P(None, None, None, "group", None),
            P(None, None, None, "group", None),
            P(),
            P(),
        ),
        out_specs=P("group", "row", None, None),
        check_vma=False,
    )
```

profile of v0, /device:TPU:28, one launch (start us, length us, event | category | flops | bytes accessed | tf_op | source)
XLA Modules:
  0.0 274.7 jit_solution(8946432891618594731)
XLA Ops:
  6.5 0.7 all-gather.3.cloned.1.call-update
  7.3 0.7 all-gather.5.cloned.1.call-update
  8.7 0.4 fusion.34
  9.1 0.8 fusion.39
  9.9 0.1 constant_dynamic-slice_fusion.1
  10.0 1.3 collective-permute-start
  12.0 0.2 reduce-window.8
  12.2 0.1 select_reduce_fusion
  12.3 6.3 %collective-permute-done = bf16[2,4,32,384]{3,1,2,0:T(4,128)(2,1)S(1)} collective-permute-done((bf16[2,4,32,384]{3,1,2,0:T(4,128)(2,1)S(1)}, bf16[2,4,32,384]{3,1,2,0:T(4,128)(2,1)S(1)}, u32[]{:S(2)}, u32[]{:S(2)}) %collective-permute-start) | collective-permute-done | bytes 196640 | tf_op jit(solution)/shard_map/ppermute | solution.py:10
  18.6 0.6 fusion.46
  19.2 1.3 collective-permute-start.1
  20.5 1.5 collective-permute-start.2
  22.0 3.8 %collective-permute-done.2 = bf16[8,1,32,384]{3,1,2,0:T(2,128)(2,1)S(1)} collective-permute-done((bf16[8,1,32,384]{3,1,2,0:T(2,128)(2,1)S(1)}, bf16[8,1,32,384]{3,1,2,0:T(2,128)(2,1)S(1)}, u32[]{:S(2)}, u32[]{:S(2)}) %collective-permute-start.2) | collective-permute-done | bytes 196640 | tf_op jit(solution)/shard_map/ppermute | solution.py:23
  25.8 1.3 pad_maximum_fusion
  27.2 0.4 slice_bitcast_fusion.23
  27.6 0.5 copy.87
  28.1 0.2 pad.2.clone
  28.4 0.1 slice.79
  28.4 0.5 copy.88
  29.0 0.2 pad.4.clone
  29.2 0.1 slice.82
  29.3 0.5 copy.86
  29.8 0.2 pad.clone
  30.1 1.7 fusion.13
  31.9 1.7 fusion.14
  33.6 0.4 fusion.12
  34.0 93.4 %all-gather.3.cloned.1.call-done = bf16[3,3,3,384,384]{4,3,2,1,0:T(8,128)(2,1)} async-done(((bf16[3,3,3,48,384]{4,3,2,1,0:T(8,128)(2,1)}), bf16[3,3,3,384,384]{4,3,2,1,0:T(8,128)(2,1)}) %all-gather.3.cloned.1.call-update) | async-done | bytes 7962640 | tf_op jit(solution)/shard_map/all_gather | solution.py:84
  127.5 6.1 %fusion.10 = f32[4,48,5,384]{3,1,2,0:T(8,128)S(1)} fusion(bf16[3,3,3,384,384]{4,3,2,1,0:T(8,128)(2,1)} %all-gather.3.cloned.1.call-done, bf16[6,6,8,7,384]{4,1,3,2,0:T(8,128)(2,1)} %fusion.13), kind=kOutput, calls=%fused_computation.16 | convolution fusion | flops 2548039680 | bytes 6193152 | tf_op jit(solution)/shard_map/conv_general_dilated | solution.py:50
  133.6 3.6 %fusion.9 = f32[4,48,5,384]{3,1,2,0:T(8,128)S(1)} fusion(bf16[3,3,3,384,384]{4,3,2,1,0:T(8,128)(2,1)S(1)} %copy-done.10, bf16[6,6,8,7,384]{4,1,3,2,0:T(8,128)(2,1)S(1)} %copy-done.1), kind=kOutput, calls=%fused_computation.14 | convolution fusion | flops 2548039680 | bytes 6193152 | tf_op jit(solution)/shard_map/conv_general_dilated | solution.py:50
  137.3 0.3 broadcast.71
  137.6 0.3 broadcast.68
  137.8 0.1 copy-done.12
  138.0 4.3 %multiply_reduce_fusion = (f32[4,48,5]{1,2,0:T(8,128)S(1)}, f32[4,48,5,384]{3,1,2,0:T(8,128)S(1)}) fusion(f32[4,48,5,384]{3,1,2,0:T(8,128)S(1)} %fusion.9, f32[4,48,5,384]{3,0,2,1:T(4,128)S(1)} %bitcast.109, f32[4,48,5,384]{3,1,2,0:T(8,128)S(1)} %fusion.10, f32[4,48,5,384]{3,0,2,1:T(4,128)S(1)} %bitcast.111, ...), kind=kOutput, calls=%fused_computation.43 | convolution fusion | flops 2551356416 | bytes 12096256 | tf_op jit(solution)/shard_map/conv_general_dilated | solution.py:50
  142.3 0.6 copy.73
  142.9 0.1 copy.74
  143.0 0.1 reshape.87
  143.1 0.1 copy.75
  143.3 0.7 fusion.44
  144.0 0.1 constant_dynamic-slice_fusion
  144.1 1.3 collective-permute-start.3
  145.4 10.4 %collective-permute-done.3 = bf16[2,4,32,384]{3,1,2,0:T(4,128)(2,1)S(1)} collective-permute-done((bf16[2,4,32,384]{3,1,2,0:T(4,128)(2,1)S(1)}, bf16[2,4,32,384]{3,1,2,0:T(4,128)(2,1)S(1)}, u32[]{:S(2)}, u32[]{:S(2)}) %collective-permute-start.3) | collective-permute-done | bytes 196640 | tf_op jit(solution)/shard_map/ppermute | solution.py:10
  155.8 0.8 fusion.45
  156.6 1.8 collective-permute-start.4
  158.5 1.3 collective-permute-start.5
  159.8 3.4 %collective-permute-done.5 = bf16[8,1,32,384]{3,1,2,0:T(2,128)(2,1)S(1)} collective-permute-done((bf16[8,1,32,384]{3,1,2,0:T(2,128)(2,1)S(1)}, bf16[8,1,32,384]{3,1,2,0:T(2,128)(2,1)S(1)}, u32[]{:S(2)}, u32[]{:S(2)}) %collective-permute-start.5) | collective-permute-done | bytes 196640 | tf_op jit(solution)/shard_map/ppermute | solution.py:23
  163.2 1.3 pad_maximum_fusion.1
  164.5 0.4 slice_bitcast_fusion.19
  164.9 0.5 copy.89
  165.5 0.2 pad.6.clone
  165.7 0.1 slice.89
  165.8 0.5 copy.90
  166.3 0.2 pad.8.clone
  166.6 0.5 copy.91
  167.2 0.2 pad.10.clone
  167.5 0.4 fusion.15
  167.9 1.7 fusion.16
  169.6 1.8 fusion.17
  171.4 80.4 %all-gather.5.cloned.1.call-done = bf16[3,3,3,384,384]{4,3,2,1,0:T(8,128)(2,1)} async-done(((bf16[3,3,3,48,384]{4,3,2,1,0:T(8,128)(2,1)}), bf16[3,3,3,384,384]{4,3,2,1,0:T(8,128)(2,1)}) %all-gather.5.cloned.1.call-update) | async-done | bytes 7962640 | tf_op jit(solution)/shard_map/all_gather | solution.py:88
  251.8 6.1 %fusion.7 = f32[4,48,5,384]{3,1,2,0:T(8,128)S(1)} fusion(bf16[3,3,3,384,384]{4,3,2,1,0:T(8,128)(2,1)} %all-gather.5.cloned.1.call-done, bf16[6,6,8,7,384]{4,1,3,2,0:T(8,128)(2,1)} %fusion.16), kind=kOutput, calls=%fused_computation.10 | convolution fusion | flops 2548039680 | bytes 6193152 | tf_op jit(solution)/shard_map/conv_general_dilated | solution.py:50
  258.0 3.6 %fusion.6 = f32[4,48,5,384]{3,1,2,0:T(8,128)S(1)} fusion(bf16[3,3,3,384,384]{4,3,2,1,0:T(8,128)(2,1)S(1)} %copy-done.9, bf16[6,6,8,7,384]{4,1,3,2,0:T(8,128)(2,1)S(1)} %copy-done.2), kind=kOutput, calls=%fused_computation.8 | convolution fusion | flops 2548039680 | bytes 6193152 | tf_op jit(solution)/shard_map/conv_general_dilated | solution.py:50
  261.7 4.2 %select_add_fusion = f32[4,48,5,384]{3,1,2,0:T(8,128)S(1)} fusion(f32[4,48,5,384]{3,1,2,0:T(8,128)S(1)} %fusion.6, f32[4,48,5,384]{3,1,2,0:T(8,128)S(1)} %fusion.7, f32[4,48,5,384]{3,0,2,1:T(4,128)S(1)} %bitcast.110, f32[4,48,5,384]{3,0,2,1:T(4,128)S(1)} %bitcast.112, bf16[3,3,3,384,384]{4,3,2,1,0:T(8,128)(2,1)S(1)} %copy-done.9, ...), kind=kOutput, calls=%fused_computation.42 | convolution fusion | flops 2550620160 | bytes 12092416 | tf_op jit(solution)/shard_map/conv_general_dilated | solution.py:50
  265.9 0.6 copy.84
  266.5 0.5 fusion.41
  267.0 0.9 copy.85
  (38 shorter events, 0.3 us)
Async XLA Ops:
  6.5 2.1 copy-start
  6.5 2.6 copy-start.7
  6.5 120.9 %all-gather.3.cloned.1.call-start = ((), (), s32[]{:S(2)}) async-start(), calls=%async_computation | async-start | bytes 8957952 | tf_op jit(solution)/shard_map/all_gather | solution.py:84
  7.3 4.7 %copy-start.11 = (s32[3]{0:T(128)S(1)}, s32[3]{0:T(128)}, u32[]{:S(2)}) copy-start(s32[3]{0:T(128)} %param.9) | copy-start | bytes 40
  7.3 244.6 %all-gather.5.cloned.1.call-start = ((), (), s32[]{:S(2)}) async-start(), calls=%async_computation.1 | async-start | bytes 8957952 | tf_op jit(solution)/shard_map/all_gather | solution.py:88
  10.0 8.5 %collective-permute-start = (bf16[2,4,32,384]{3,1,2,0:T(4,128)(2,1)S(1)}, bf16[2,4,32,384]{3,1,2,0:T(4,128)(2,1)S(1)}, u32[]{:S(2)}, u32[]{:S(2)}) collective-permute-start(bf16[2,4,32,384]{3,1,2,0:T(4,128)(2,1)S(1)} %constant_dynamic-slice_fusion.1), channel_id=1, source_target_pairs={{0,4},{4,8},{8,12},{12,16},{16,20},{20,24},{24,28},{1,5},{5,9},{9,... | collective-permute-start | bytes 589832 | tf_op jit(solution)/shard_map/ppermute | solution.py:10
  19.2 2.8 %collective-permute-start.1 = (bf16[8,1,32,384]{3,1,2,0:T(2,128)(2,1)S(1)}, bf16[8,1,32,384]{3,1,2,0:T(2,128)(2,1)S(1)}, u32[]{:S(2)}, u32[]{:S(2)}) collective-permute-start(bf16[8,1,32,384]{3,1,2,0:T(2,128)(2,1)S(1)} %get-tuple-element.13), channel_id=1, source_target_pairs={{0,1},{1,2},{2,3},{4,5},{5,6},{6,7},{8,9},{9,10},{10,11},{12,13},{... | collective-permute-start | bytes 589832 | tf_op jit(solution)/shard_map/ppermute | solution.py:21
  20.5 5.3 %collective-permute-start.2 = (bf16[8,1,32,384]{3,1,2,0:T(2,128)(2,1)S(1)}, bf16[8,1,32,384]{3,1,2,0:T(2,128)(2,1)S(1)}, u32[]{:S(2)}, u32[]{:S(2)}) collective-permute-start(bf16[8,1,32,384]{3,1,2,0:T(2,128)(2,1)S(1)} %get-tuple-element.14), channel_id=1, source_target_pairs={{1,0},{2,1},{3,2},{5,4},{6,5},{7,6},{9,8},{10,9},{11,10},{13,12},{... | collective-permute-start | bytes 589832 | tf_op jit(solution)/shard_map/ppermute | solution.py:23
  127.5 6.2 %copy-start.1 = (bf16[6,6,8,7,384]{4,1,3,2,0:T(8,128)(2,1)S(1)}, bf16[6,6,8,7,384]{4,1,3,2,0:T(8,128)(2,1)}, u32[]{:S(2)}) copy-start(bf16[6,6,8,7,384]{4,1,3,2,0:T(8,128)(2,1)} %fusion.14) | copy-start | bytes 4644868
  127.5 6.2 %copy-start.10 = (bf16[3,3,3,384,384]{4,3,2,1,0:T(8,128)(2,1)S(1)}, bf16[3,3,3,384,384]{4,3,2,1,0:T(8,128)(2,1)}, u32[]{:S(2)}) copy-start(bf16[3,3,3,384,384]{4,3,2,1,0:T(8,128)(2,1)} %all-gather.3.cloned.1.call-done) | copy-start | bytes 23887876
  137.3 0.7 copy-start.12
  137.5 4.7 %copy-start.3 = (f32[4,6,40,384]{3,0,2,1:T(4,128)}, f32[4,6,40,384]{3,0,2,1:T(4,128)S(1)}, u32[]{:S(2)}) copy-start(f32[4,6,40,384]{3,0,2,1:T(4,128)S(1)} %broadcast.71) | copy-start | bytes 4423684
  137.8 4.5 %copy-start.5 = (f32[4,6,40,384]{3,0,2,1:T(4,128)}, f32[4,6,40,384]{3,0,2,1:T(4,128)S(1)}, u32[]{:S(2)}) copy-start(f32[4,6,40,384]{3,0,2,1:T(4,128)S(1)} %broadcast.68) | copy-start | bytes 4423684
  142.3 1.0 copy-start.8
  144.1 11.7 %collective-permute-start.3 = (bf16[2,4,32,384]{3,1,2,0:T(4,128)(2,1)S(1)}, bf16[2,4,32,384]{3,1,2,0:T(4,128)(2,1)S(1)}, u32[]{:S(2)}, u32[]{:S(2)}) collective-permute-start(bf16[2,4,32,384]{3,1,2,0:T(4,128)(2,1)S(1)} %constant_dynamic-slice_fusion), channel_id=1, source_target_pairs={{0,4},{4,8},{8,12},{12,16},{16,20},{20,24},{24,28},{1,5},{5,9},{9,... | collective-permute-start | bytes 589832 | tf_op jit(solution)/shard_map/ppermute | solution.py:10
  156.6 3.2 %collective-permute-start.4 = (bf16[8,1,32,384]{3,1,2,0:T(2,128)(2,1)S(1)}, bf16[8,1,32,384]{3,1,2,0:T(2,128)(2,1)S(1)}, u32[]{:S(2)}, u32[]{:S(2)}) collective-permute-start(bf16[8,1,32,384]{3,1,2,0:T(2,128)(2,1)S(1)} %get-tuple-element.11), channel_id=1, source_target_pairs={{0,1},{1,2},{2,3},{4,5},{5,6},{6,7},{8,9},{9,10},{10,11},{12,13},{... | collective-permute-start | bytes 589832 | tf_op jit(solution)/shard_map/ppermute | solution.py:21
  158.5 4.8 %collective-permute-start.5 = (bf16[8,1,32,384]{3,1,2,0:T(2,128)(2,1)S(1)}, bf16[8,1,32,384]{3,1,2,0:T(2,128)(2,1)S(1)}, u32[]{:S(2)}, u32[]{:S(2)}) collective-permute-start(bf16[8,1,32,384]{3,1,2,0:T(2,128)(2,1)S(1)} %get-tuple-element.12), channel_id=1, source_target_pairs={{1,0},{2,1},{3,2},{5,4},{6,5},{7,6},{9,8},{10,9},{11,10},{13,12},{... | collective-permute-start | bytes 589832 | tf_op jit(solution)/shard_map/ppermute | solution.py:23
  251.8 6.2 %copy-start.2 = (bf16[6,6,8,7,384]{4,1,3,2,0:T(8,128)(2,1)S(1)}, bf16[6,6,8,7,384]{4,1,3,2,0:T(8,128)(2,1)}, u32[]{:S(2)}) copy-start(bf16[6,6,8,7,384]{4,1,3,2,0:T(8,128)(2,1)} %fusion.17) | copy-start | bytes 4644868
  251.8 6.2 %copy-start.9 = (bf16[3,3,3,384,384]{4,3,2,1,0:T(8,128)(2,1)S(1)}, bf16[3,3,3,384,384]{4,3,2,1,0:T(8,128)(2,1)}, u32[]{:S(2)}) copy-start(bf16[3,3,3,384,384]{4,3,2,1,0:T(8,128)(2,1)} %all-gather.5.cloned.1.call-done) | copy-start | bytes 23887876
  258.0 3.7 %copy-start.4 = (f32[4,6,40,384]{3,0,2,1:T(4,128)S(1)}, f32[4,6,40,384]{3,0,2,1:T(4,128)}, u32[]{:S(2)}) copy-start(f32[4,6,40,384]{3,0,2,1:T(4,128)} %copy-done.3) | copy-start | bytes 4423684
  258.0 3.7 %copy-start.6 = (f32[4,6,40,384]{3,0,2,1:T(4,128)S(1)}, f32[4,6,40,384]{3,0,2,1:T(4,128)}, u32[]{:S(2)}) copy-start(f32[4,6,40,384]{3,0,2,1:T(4,128)} %copy-done.5) | copy-start | bytes 4423684
Sparse Core Ops, SparseCore 0:
  9.6 117.8 all-gather.2
  129.7 122.0 all-gather.4
where the time goes:
time: 280 us; the launch traced here: 275 us
  waiting for transfers between devices  199 us (71%)
  matrix products  28.1 us (10%)
  between operations  15.2 us (5%)
  other arithmetic  14.6 us (5%)
  local copies, waits for them, and re-layouts  9.06 us (3%)
  starting transfers between devices  8.54 us (3%)
    all_gather x1, waiting for transfers between devices, per_device(): lax.all_gather(kernel_one, 'group', axis=3, tiled=True)  93.4 us
    all_gather x1, waiting for transfers between devices, per_device(): lax.all_gather(kernel_two, 'group', axis=3, tiled=True)  80.4 us
    conv_general_dilated x6, matrix products, spatial_taps(): lax.conv_general_dilated(window, kernel_piece[lag_index], (1, 1), ((0, 0)...  28.1 us
    ppermute x2, waiting for transfers between devices, passed_along(): return lax.ppermute(array, axis, pairs)  16.7 us
    conv_general_dilated x6, other arithmetic, spatial_taps(): lax.conv_general_dilated(window, kernel_piece[lag_index], (1, 1), ((0, 0)...  7.78 us
    ppermute x2, waiting for transfers between devices, with_halo(): lax.ppermute(head, axis, [((i + 1) % count, i) for i in range(ends)])  7.26 us
  transfers between devices with their start and end apart: 8, of which 6 were waited for; matrix products, arithmetic and copies ran while one was open for 13% of the time, Pallas kernels for 0%

commit v1 on v0

v1 whole, which is shorter than its diff:
```python
import functools
import math

import jax
import jax.numpy as jnp
from jax import lax
from jax.experimental import pallas as pl
from jax.experimental.pallas import tpu as pltpu
from jax.sharding import PartitionSpec as P

MESH = pl.DeviceIdType.MESH
BF16 = jnp.bfloat16
F32 = jnp.float32


def clip_positions(clip_lengths, frame_index):
    ends = jnp.cumsum(clip_lengths)
    begins = jnp.max(jnp.where(ends[None, :] <= frame_index[:, None], ends[None, :], 0), axis=1)
    return frame_index - begins


def norm_act(data, gain):
    mean_square = jnp.mean(data * data, axis=-1, keepdims=True)
    scaled = data * lax.rsqrt(mean_square + 1e-06) * gain
    return (scaled / (1.0 + jnp.exp(-scaled))).astype(BF16)


def kernel(
    layout, gathers,
    frames, k1, k2, gain1, gain2, masks, live, count,
    out,
    w1, w2, act, last, pad, a3, acc,
    piece_recv, piece_send, halo_recv, halo_send, own_sem,
):
    nz, ny, nr = layout
    ng = nz * ny
    slots, rows, cols, ch = frames.shape
    per = rows * cols
    g, r = lax.axis_index("group"), lax.axis_index("row")
    z, y = g // ny, g % ny
    x, c = r // 2, r % 2
    weights = (w1, w2)
    kernels = (k1, k2)
    pending = []

    always = g >= 0
    up = (z < nz - 1, g + ny, r)
    down = (z > 0, g - ny, r)
    across = (always, z * ny + (1 - y), r)
    sibling = (always, g, x * 2 + (1 - c))
    other = (always, g, (1 - x) * 2 + (1 - c))

    greet = []
    if gathers:
        greet += [up, down, across, sibling, other]
    for dr in (-1, 0, 1):
        ok_r = jnp.logical_and(r + dr >= 0, r + dr < nr)
        for dg in (-1, 0, 1):
            if dr == 0 and dg == 0:
                continue
            ok = jnp.logical_and(ok_r, jnp.logical_and(g + dg >= 0, g + dg < ng))
            greet.append((ok, g + dg, r + dr))
    barrier = pltpu.get_barrier_semaphore()
    total = 0
    for ok, tg, tr in greet:
        @pl.when(ok)
        def _(tg=tg, tr=tr):
            pl.semaphore_signal(barrier, inc=1, device_id=(tg, tr), device_id_type=MESH)
        total = total + ok.astype(jnp.int32)
    pl.semaphore_wait(barrier, total)

    def send(ok, src, dst, ssem, rsem, tg, tr):
        copy = pltpu.make_async_remote_copy(
            src_ref=src, dst_ref=dst, send_sem=ssem, recv_sem=rsem,
            device_id=(tg, tr), device_id_type=MESH,
        )

        @pl.when(ok)
        def _():
            copy.start()
        pending.append((ok, copy))

    if gathers:
        depth = k1.shape[3]
        mine = 2 * c + (1 - c) * x

        def piece(i, t, s):
            return weights[i].at[t, :, :, pl.ds(pl.multiple_of(s * depth, depth), depth), :]

        def send_piece(i, t, s, way, ok, to, src=None):
            there = piece(i, t, s)
            send(
                ok, there if src is None else src, there,
                piece_send.at[i, s, way], piece_recv.at[i, t, s], to[1], to[2],
            )

        def wait_piece(i, t, s, ok):
            there = piece(i, t, s)

            @pl.when(ok)
            def _():
                pltpu.make_async_remote_copy(
                    src_ref=there, dst_ref=there, send_sem=piece_send.at[i, s, 0],
                    recv_sem=piece_recv.at[i, t, s], device_id=(g, sibling[2]),
                    device_id_type=MESH,
                ).wait_recv()

        def land_own(i):
            return pltpu.make_async_copy(
                kernels[i],
                weights[i].at[:, :, :, pl.ds(pl.multiple_of(g * depth, depth), depth), :],
                own_sem.at[i],
            )

        def start_own(i):
            src = kernels[i].at[mine]
            send_piece(i, mine, g, 0, up[0], up, src)
            send_piece(i, mine, g, 1, down[0], down, src)
            send_piece(i, mine, g, 2, always, across, src)

        def both(a, b):
            return jnp.logical_and(a, b)

        def arrivals(step):
            kind, d = step
            row_y = y if kind == "z" else 1 - y
            found = []
            for sign in ((-1, 1) if d else (1,)):
                zz = z + sign * d
                ok = both(zz >= 0, zz < nz)
                s = jnp.clip(zz, 0, nz - 1) * ny + row_y
                found.append((ok, s, sign))
            return found

        steps = [("z", 1), ("y", 0)]
        for d in range(2, nz):
            steps += [("z", d), ("y", d - 1)]
        steps += [("y", nz - 1)]

        def relay(i, step):
            for ok, s, sign in arrivals(step):
                wait_piece(i, mine, s, ok)
                if step[0] == "z":
                    if sign < 0:
                        send_piece(i, mine, s, 0, both(ok, up[0]), up)
                    else:
                        send_piece(i, mine, s, 1, both(ok, down[0]), down)
                    send_piece(i, mine, s, 2, ok, across)
                send_piece(i, mine, s, 3, both(ok, c == 0), other)
                send_piece(i, mine, s, 4, ok, sibling)

        def relay_crossed(i, step):
            for ok, s, _ in arrivals(step):
                here = both(ok, c == 1)
                wait_piece(i, 1 - x, s, here)
                send_piece(i, 1 - x, s, 5, here, sibling)

        def full(i, n):
            relay(i, steps[n])
            if n:
                relay_crossed(i, steps[n - 1])

        def finish(i):
            relay_crossed(i, steps[-1])
            for step in steps:
                for ok, s, _ in arrivals(step):
                    wait_piece(i, 2 * (1 - c) + c * x, s, ok)
                    wait_piece(i, 1 - x, s, both(ok, c == 0))
            land_own(i).wait()

        land_own(0).start()
        land_own(1).start()
        start_own(0)

    def share_edges(i, read, gain):
        for s in range(slots):
            done = norm_act(read(s), gain[...]).reshape(rows, cols, ch)
            act[i, s] = done
            pad[i, 2 + s, 1 : 1 + rows] = done
        last[i] = act[i, pl.ds(jnp.clip(count[0] - 2, 0, slots - 2), 2)]

        @pl.when(r == 0)
        def _():
            pad[i, :, 0] = jnp.zeros((slots + 2, cols, ch), BF16)

        @pl.when(r == nr - 1)
        def _():
            pad[i, :, rows + 1] = jnp.zeros((slots + 2, cols, ch), BF16)

        @pl.when(g == 0)
        def _():
            pad[i, 0:2] = jnp.zeros((2, rows + 2, cols, ch), BF16)

        mine_in = pad.at[i]
        below, above, after = r < nr - 1, r > 0, g < ng - 1
        whole = pl.ds(2, slots)
        two = pl.ds(0, 2)
        plan = [
            (below, act.at[i, :, rows - 1], mine_in.at[whole, 0], g, r + 1, r > 0),
            (above, act.at[i, :, 0], mine_in.at[whole, rows + 1], g, r - 1, r < nr - 1),
            (after, last.at[i], mine_in.at[two, pl.ds(1, rows)], g + 1, r, g > 0),
            (
                jnp.logical_and(after, below), last.at[i, :, rows - 1],
                mine_in.at[two, 0], g + 1, r + 1, jnp.logical_and(g > 0, r > 0),
            ),
            (
                jnp.logical_and(after, above), last.at[i, :, 0],
                mine_in.at[two, rows + 1], g + 1, r - 1, jnp.logical_and(g > 0, r < nr - 1),
            ),
        ]
        waits = []
        for n, (ok, src, dst, tg, tr, comes) in enumerate(plan):
            send(ok, src, dst, halo_send.at[i, n], halo_recv.at[i, n], tg, tr)
            waits.append((comes, pending[-1][1]))
        return waits

    def gather_columns(i, waits):
        for comes, copy in waits:
            @pl.when(comes)
            def _(copy=copy):
                copy.wait_recv()
        size = (rows + 2) * cols
        col = lax.broadcasted_iota(jnp.int32, (size, ch), 0) % cols

        def body(f, carry):
            middle = pad[i, f].reshape(size, ch)
            wide = middle.astype(F32)
            left = jnp.where(col == 0, 0.0, pltpu.roll(wide, 1, 0)).astype(BF16)
            right = jnp.where(col == cols - 1, 0.0, pltpu.roll(wide, size - 1, 0)).astype(BF16)
            shape = (rows + 2, cols, ch)
            a3[f, :, :, 0:ch] = left.reshape(shape)
            a3[f, :, :, ch : 2 * ch] = middle.reshape(shape)
            a3[f, :, :, 2 * ch : 3 * ch] = right.reshape(shape)
            return carry

        lax.fori_loop(0, slots + 2, body, 0)

    def clear():
        acc[...] = jnp.zeros(acc.shape, F32)

    def taps(i, t):
        def body(p, carry):
            lhs = a3[pl.ds(t, slots), pl.ds(p, rows)].reshape(slots * per, 3 * ch)
            rhs = weights[i][t, p].reshape(3 * ch, ch)
            part = jnp.dot(lhs, rhs, preferred_element_type=F32)
            for s in range(slots):
                acc[s] += part[s * per : (s + 1) * per] * masks[t * slots + s]
            return carry

        lax.fori_loop(0, 3, body, 0)

    if not gathers:
        weights = (k1, k2)
    waits = share_edges(0, lambda s: frames[s].reshape(per, ch).astype(F32), gain1)
    if gathers:
        full(0, 0)
    gather_columns(0, waits)
    clear()
    if gathers:
        for n in range(1, len(steps)):
            full(0, n)
            if n == 3:
                start_own(1)
        full(1, 0)
        finish(0)
    for t in range(3):
        taps(0, t)
        if gathers:
            full(1, t + 1)
    waits = share_edges(1, lambda s: acc[s], gain2)
    if gathers:
        full(1, 4)
    gather_columns(1, waits)
    clear()
    if gathers:
        for n in range(5, len(steps)):
            full(1, n)
        finish(1)

    def second(t, carry):
        taps(1, t)
        return carry

    lax.fori_loop(0, 3, second, 0)
    for s in range(slots):
        summed = frames[s].reshape(per, ch).astype(F32) + acc[s]
        kept = jnp.where(jnp.full(summed.shape, live[s], F32) > 0.0, summed, 0.0)
        out[s] = kept.astype(BF16).reshape(rows, cols, ch)
    for ok, copy in pending:
        @pl.when(ok)
        def _(copy=copy):
            copy.wait_send()


def per_device(
    layout, frames, clip_lengths, group_start, group_count, kernel_one, kernel_two, gain_one, gain_two
):
    nz, ny, nr = layout
    slots, rows, cols, ch = frames.shape
    depth = kernel_one.shape[3]
    gathers = depth % 16 == 0 and ny == 2 and nr == 4
    position = clip_positions(clip_lengths, group_start[0] + jnp.arange(slots, dtype=jnp.int32))
    masks = (position[None, :] >= jnp.array([2, 1, 0])[:, None]).astype(F32).reshape(-1)
    live = (jnp.arange(slots, dtype=jnp.int32) < group_count[0]).astype(F32)
    if not gathers:
        kernel_one = lax.all_gather(kernel_one, "group", axis=3, tiled=True)
        kernel_two = lax.all_gather(kernel_two, "group", axis=3, tiled=True)
    vmem = pl.BlockSpec(memory_space=pltpu.VMEM)
    smem = pl.BlockSpec(memory_space=pltpu.SMEM)
    weight_spec = pl.BlockSpec(memory_space=pl.ANY) if gathers else vmem
    full = (3, 3, 3, ch, ch) if gathers else (8, 128)
    shards = lax.axis_size("group")
    dma = pltpu.SemaphoreType.DMA
    return pl.pallas_call(
        functools.partial(kernel, layout, gathers),
        out_shape=jax.ShapeDtypeStruct(frames.shape, BF16),
        in_specs=[vmem, weight_spec, weight_spec, vmem, vmem, smem, smem, smem],
        out_specs=vmem,
        scratch_shapes=[
            pltpu.VMEM(full, BF16),
            pltpu.VMEM(full, BF16),
            pltpu.VMEM((2, slots, rows, cols, ch), BF16),
            pltpu.VMEM((2, 2, rows, cols, ch), BF16),
            pltpu.VMEM((2, slots + 2, rows + 2, cols, ch), BF16),
            pltpu.VMEM((slots + 2, rows + 2, cols, 3 * ch), BF16),
            pltpu.VMEM((slots, rows * cols, ch), F32),
            dma((2, 3, shards) if gathers else (1,)),
            dma((2, shards, 6) if gathers else (1,)),
            dma((2, 5)),
            dma((2, 5)),
            dma((2,)),
        ],
        compiler_params=pltpu.CompilerParams(
            collective_id=0, has_side_effects=True, vmem_limit_bytes=56 * 1024 * 1024
        ),
    )(
        frames, kernel_one, kernel_two, gain_one[None, :], gain_two[None, :], masks, live, group_count
    )


def solution(mesh):
    groups, rows = mesh.shape["group"], mesh.shape["row"]
    ny = math.isqrt(groups // 2)
    return jax.shard_map(
        functools.partial(per_device, (groups // ny, ny, rows)),
        mesh=mesh,
        in_specs=(
            P("group", "row", None, None),
            P(),
            P("group"),
            P("group"),
            P(None, None, None, "group", None),
            P(None, None, None, "group", None),
            P(),
            P(),
        ),
        out_specs=P("group", "row", None, None),
        check_vma=False,
    )
```

time: 280 us -> 109 us (0.39); the launches traced: 275 us -> 109 us
  waiting for transfers between devices: 199 us -> 0 us
  Pallas kernels: 0 us -> 102 us
  matrix products: 28.1 us -> 0 us
  between operations: 15.2 us -> 1.33 us
  other arithmetic: 14.6 us -> 0.85 us
  starting transfers between devices: 8.54 us -> 0 us
  local copies, waits for them, and re-layouts: 9.06 us -> 4.7 us
    all_gather x2 -> x0, waiting for transfers between devices: 174 us -> none  [the longest x1 93.4 us: per_device(): lax.all_gather(kernel_one, 'group', axis=3, tiled=True)]
    pallas_call x0 -> x1, Pallas kernels: none -> 102 us  [per_device(): pl.pallas_call(functools.partial(kernel, layout, gathers), out_shape=jax....]
    conv_general_dilated x6 -> x0, matrix products: 28.1 us -> none  [spatial_taps(): lax.conv_general_dilated(window, kernel_piece[lag_index], (1, 1), ((0, 0)...]
    ppermute x6 -> x0, waiting for transfers between devices: 24 us -> none  [the longest x2 16.7 us: passed_along(): return lax.ppermute(array, axis, pairs)]
    ppermute x6 -> x0, starting transfers between devices: 8.5 us -> none  [the longest x2 3.16 us: with_halo(): lax.ppermute(tail, axis, [(i, (i + 1) % count) for i in range(ends)])]
    conv_general_dilated x6 -> x0, other arithmetic: 7.78 us -> none  [spatial_taps(): lax.conv_general_dilated(window, kernel_piece[lag_index], (1, 1), ((0, 0)...]
    concatenate x4 -> x0, other arithmetic: 4.06 us -> none  [the longest x2 2.62 us: with_halo(): jnp.concatenate([lax.ppermute(tail, axis, [(i, (i + 1) % count) for i in...]
  transfers between devices with their start and end apart: 8 -> 0, of which waited for: 6 -> 0; matrix products, arithmetic and copies ran while one was open for 13% -> 0% of each run, Pallas kernels for 0% -> 0%
where the time goes in v1:
time: 109 us
  Pallas kernels  102 us (94%)
  local copies, waits for them, and re-layouts  4.7 us (4%)
  between operations  1.33 us (1%)
    pallas_call x1, Pallas kernels, per_device(): pl.pallas_call(functools.partial(kernel, layout, gathers), out_shape=jax....  102 us
    unnamed x9, local copies, waits for them, and re-layouts  2.88 us

profile of v1, /device:TPU:28, one launch (start us, length us, event | category | flops | bytes accessed | tf_op | source)
XLA Modules:
  0.0 109.1 jit_solution(5877311557621303604)
XLA Ops:
  1.3 0.0 copy-start.3
  1.3 0.6 copy-done.3
  2.0 0.2 reduce-window.8
  2.1 0.1 select_reduce_fusion
  2.2 0.0 copy-start.2
  2.2 0.5 compare_convert_fusion.live
  2.8 0.1 copy-done.2
  2.9 0.1 compare_convert_fusion.1
  3.0 0.0 copy-start
  3.0 0.7 reshape.44.masks
  3.6 0.0 copy-done
  3.6 0.0 copy-start.1
  3.6 0.6 broadcast_in_dim.14.gain1
  4.2 0.1 copy-done.1
  4.3 0.6 broadcast_in_dim.22.gain2
  4.9 102.2 %shard_map.91 = bf16[6,4,32,384]{3,2,1,0:T(8,128)(2,1)} custom-call(bf16[6,4,32,384]{3,2,1,0:T(8,128)(2,1)} %frames.1, bf16[3,3,3,48,384]{4,3,2,1,0:T(8,128)(2,1)} %k1.1, bf16[3,3,3,48,384]{4,3,2,1,0:T(8,128)(2,1)} %k2.1, f32[1,384]{1,0:T(1,128)} %broadcast_in_dim.14.gain1, f32[1,384]{1,0:T(1,128)} %broadcast_in_dim.22.gain2, f32[18]{0:T(128)} %reshape.44.masks, ...), custom_call_target="tpu_custom_call" | custom-call | tf_op jit(solution)/shard_map/pallas_call | solution.py:314
  107.1 2.0 %copy.13 = bf16[6,4,32,384]{3,2,1,0:T(8,128)(2,1)} copy(bf16[6,4,32,384]{3,2,1,0:T(8,128)(2,1)} %shard_map.91) | data formatting | bytes 1179648
  (2 shorter events, 0.0 us)
Async XLA Ops:
  1.3 0.7 copy-start.3
  2.2 0.7 copy-start.2
  3.0 0.7 copy-start
  3.6 0.7 copy-start.1

commit v2 on v1

v2 whole, which is shorter than its diff:
```python
import functools
import math

import jax
import jax.numpy as jnp
from jax import lax
from jax.experimental import pallas as pl
from jax.experimental.pallas import tpu as pltpu
from jax.sharding import PartitionSpec as P

MESH = pl.DeviceIdType.MESH
BF16 = jnp.bfloat16
F32 = jnp.float32


def norm_act(data, gain):
    mean_square = jnp.mean(data * data, axis=-1, keepdims=True)
    scaled = data * lax.rsqrt(mean_square + 1e-06) * gain
    return (scaled / (1.0 + jnp.exp(-scaled))).astype(BF16)


def kernel(
    layout, gathers,
    frames, k1, k2, gain1, gain2, lengths, start, count,
    out,
    w, act, last, pad, a3, acc,
    piece_recv, piece_send, halo_recv, halo_send, own_sem,
):
    nz, ny, nr = layout
    ng = nz * ny
    slots, rows, cols, ch = frames.shape
    per = rows * cols
    g, r = lax.axis_index("group"), lax.axis_index("row")
    z, y = g // ny, g % ny
    x, c = r // 2, r % 2
    kernels = (k1, k2)
    pending = []

    always = g >= 0
    up = (z < nz - 1, g + ny, r)
    down = (z > 0, g - ny, r)
    across = (always, z * ny + (1 - y), r)
    sibling = (always, g, x * 2 + (1 - c))
    other = (always, g, (1 - x) * 2 + (1 - c))

    greet = []
    if gathers:
        greet += [up, down, across, sibling, other]
    for dr in (-1, 0, 1):
        ok_r = jnp.logical_and(r + dr >= 0, r + dr < nr)
        for dg in (-1, 0, 1):
            if dr == 0 and dg == 0:
                continue
            ok = jnp.logical_and(ok_r, jnp.logical_and(g + dg >= 0, g + dg < ng))
            greet.append((ok, g + dg, r + dr))
    if gathers:
        depth = k1.shape[3]
        own = pl.ds(pl.multiple_of(g * depth, depth), depth)
        landings = [
            pltpu.make_async_copy(
                kernels[n // 3].at[:, n % 3], w.at[n, :, :, own, :], own_sem.at[n]
            )
            for n in range(6)
        ]
        for landing in landings:
            landing.start()
    barrier = pltpu.get_barrier_semaphore()
    total = 0
    for ok, tg, tr in greet:
        @pl.when(ok)
        def _(tg=tg, tr=tr):
            pl.semaphore_signal(barrier, inc=1, device_id=(tg, tr), device_id_type=MESH)
        total = total + ok.astype(jnp.int32)
    pl.semaphore_wait(barrier, total)

    def send(ok, src, dst, ssem, rsem, tg, tr):
        copy = pltpu.make_async_remote_copy(
            src_ref=src, dst_ref=dst, send_sem=ssem, recv_sem=rsem,
            device_id=(tg, tr), device_id_type=MESH,
        )

        @pl.when(ok)
        def _():
            copy.start()
        pending.append((ok, copy))

    if gathers:
        mine = 2 * c + (1 - c) * x

        def piece(n, t, s):
            return w.at[n, t, :, pl.ds(pl.multiple_of(s * depth, depth), depth), :]

        def piece_copy(n, t, s, way, to):
            there = piece(n, t, s)
            return pltpu.make_async_remote_copy(
                src_ref=there, dst_ref=there, send_sem=piece_send.at[n, s, way],
                recv_sem=piece_recv.at[n, t, s], device_id=(to[1], to[2]),
                device_id_type=MESH,
            )

        def send_piece(n, t, s, way, ok, to):
            @pl.when(ok)
            def _():
                piece_copy(n, t, s, way, to).start()

        def sent_piece(n, t, s, way, ok, to):
            @pl.when(ok)
            def _():
                piece_copy(n, t, s, way, to).wait_send()

        def wait_piece(n, t, s, ok):
            @pl.when(ok)
            def _():
                piece_copy(n, t, s, 0, sibling).wait_recv()

        def both(a, b):
            return jnp.logical_and(a, b)

        def own_pieces(n, act_on):
            act_on(n, mine, g, 0, up[0], up)
            act_on(n, mine, g, 1, down[0], down)
            act_on(n, mine, g, 2, always, across)

        def arrivals(step):
            kind, d = step
            row_y = y if kind == "z" else 1 - y
            found = []
            for sign in ((-1, 1) if d else (1,)):
                zz = z + sign * d
                ok = both(zz >= 0, zz < nz)
                s = jnp.clip(zz, 0, nz - 1) * ny + row_y
                found.append((ok, s, sign))
            return found

        steps = [("z", 1), ("y", 0)]
        for d in range(2, nz):
            steps += [("z", d), ("y", d - 1)]
        steps += [("y", nz - 1)]

        def passed_on(n, step, ok, s, sign, act_on):
            if step[0] == "z":
                if sign < 0:
                    act_on(n, mine, s, 0, both(ok, up[0]), up)
                else:
                    act_on(n, mine, s, 1, both(ok, down[0]), down)
                act_on(n, mine, s, 2, ok, across)
            act_on(n, mine, s, 3, both(ok, c == 0), other)
            act_on(n, mine, s, 4, ok, sibling)

        def relay(n, k):
            for ok, s, sign in arrivals(steps[k]):
                wait_piece(n, mine, s, ok)
                passed_on(n, steps[k], ok, s, sign, send_piece)

        def cross(n, k):
            for ok, s, _ in arrivals(steps[k]):
                here = both(ok, c == 1)
                wait_piece(n, 1 - x, s, here)
                send_piece(n, 1 - x, s, 5, here, sibling)

        def finish(n):
            for step in steps:
                for ok, s, _ in arrivals(step):
                    wait_piece(n, 2 * (1 - c) + c * x, s, ok)
                    wait_piece(n, 1 - x, s, both(ok, c == 0))

        def drain(n, carry):
            own_pieces(n, sent_piece)
            for step in steps:
                for ok, s, sign in arrivals(step):
                    passed_on(n, step, ok, s, sign, sent_piece)
                    sent_piece(n, 1 - x, s, 5, both(ok, c == 1), sibling)
            return carry

        for landing in landings:
            landing.wait()
        own_pieces(0, send_piece)

    def share_edges(i, read, gain):
        for s in range(slots):
            done = norm_act(read(s), gain[...][None, :]).reshape(rows, cols, ch)
            act[i, s] = done
            pad[i, 2 + s, 1 : 1 + rows] = done
        last[i] = act[i, pl.ds(jnp.clip(count[0] - 2, 0, slots - 2), 2)]

        @pl.when(r == 0)
        def _():
            pad[i, :, 0] = jnp.zeros((slots + 2, cols, ch), BF16)

        @pl.when(r == nr - 1)
        def _():
            pad[i, :, rows + 1] = jnp.zeros((slots + 2, cols, ch), BF16)

        @pl.when(g == 0)
        def _():
            pad[i, 0:2] = jnp.zeros((2, rows + 2, cols, ch), BF16)

        mine_in = pad.at[i]
        below, above, after = r < nr - 1, r > 0, g < ng - 1
        whole = pl.ds(2, slots)
        two = pl.ds(0, 2)
        plan = [
            (below, act.at[i, :, rows - 1], mine_in.at[whole, 0], g, r + 1, r > 0),
            (above, act.at[i, :, 0], mine_in.at[whole, rows + 1], g, r - 1, r < nr - 1),
            (after, last.at[i], mine_in.at[two, pl.ds(1, rows)], g + 1, r, g > 0),
            (
                jnp.logical_and(after, below), last.at[i, :, rows - 1],
                mine_in.at[two, 0], g + 1, r + 1, jnp.logical_and(g > 0, r > 0),
            ),
            (
                jnp.logical_and(after, above), last.at[i, :, 0],
                mine_in.at[two, rows + 1], g + 1, r - 1, jnp.logical_and(g > 0, r < nr - 1),
            ),
        ]
        waits = []
        for n, (ok, src, dst, tg, tr, comes) in enumerate(plan):
            send(ok, src, dst, halo_send.at[i, n], halo_recv.at[i, n], tg, tr)
            waits.append((comes, pending[-1][1]))
        return waits

    def gather_columns(i, waits):
        for comes, copy in waits:
            @pl.when(comes)
            def _(copy=copy):
                copy.wait_recv()
        size = (rows + 2) * cols
        col = lax.broadcasted_iota(jnp.int32, (size, ch), 0) % cols

        def body(f, carry):
            middle = pad[i, f].reshape(size, ch)
            wide = middle.astype(F32)
            left = jnp.where(col == 0, 0.0, pltpu.roll(wide, 1, 0)).astype(BF16)
            right = jnp.where(col == cols - 1, 0.0, pltpu.roll(wide, size - 1, 0)).astype(BF16)
            shape = (rows + 2, cols, ch)
            a3[f, :, :, 0:ch] = left.reshape(shape)
            a3[f, :, :, ch : 2 * ch] = middle.reshape(shape)
            a3[f, :, :, 2 * ch : 3 * ch] = right.reshape(shape)
            return carry

        lax.fori_loop(0, slots + 2, body, 0)

    def clear():
        acc[...] = jnp.zeros(acc.shape, F32)

    position = []
    for s in range(slots):
        frame = start[0] + s
        begin, end = jnp.int32(0), jnp.int32(0)
        for m in range(lengths.shape[0]):
            end = end + lengths[m]
            begin = jnp.where(end <= frame, jnp.maximum(begin, end), begin)
        position.append(frame - begin)

    def taps(i, p, t):
        lhs = a3[t : t + slots, pl.ds(p, rows)].reshape(slots * per, 3 * ch)
        held = w[3 * i + p, t] if gathers else kernels[i][t, p]
        part = jnp.dot(lhs, held.reshape(3 * ch, ch), preferred_element_type=F32)
        for s in range(slots):
            here = part[s * per : (s + 1) * per]
            if t < 2:
                here = here * jnp.where(position[s] >= 2 - t, 1.0, 0.0)
            acc[s] += here

    def read_frame(s):
        return frames[s].reshape(per, ch).astype(F32)

    def phase(i, n, carry=0):
        relay(n, 0)
        cross(n - 1, 5)
        relay(n, 1)
        cross(n - 1, 6)
        finish(n - 1)
        taps(i, n - 1 - 3 * i, 0)
        relay(n, 2)
        cross(n, 0)

        @pl.when(n < 5)
        def _():
            own_pieces(n + 1, send_piece)
        taps(i, n - 1 - 3 * i, 1)
        relay(n, 3)
        cross(n, 1)
        taps(i, n - 1 - 3 * i, 2)
        for k in range(4, 7):
            relay(n, k)
            cross(n, k - 2)
        return carry

    def all_taps(i):
        def body(p, carry):
            for t in range(3):
                taps(i, p, t)
            return carry

        lax.fori_loop(0, 3, body, 0)

    if gathers:
        waits = share_edges(0, read_frame, gain1)
        relay(0, 0)
        relay(0, 1)
        gather_columns(0, waits)
        clear()
        relay(0, 2)
        cross(0, 0)
        own_pieces(1, send_piece)
        for k in range(3, 7):
            relay(0, k)
            cross(0, k - 2)
        lax.fori_loop(1, 3, functools.partial(phase_of, phase, 0), 0)
        relay(3, 0)
        cross(2, 5)
        relay(3, 1)
        cross(2, 6)
        finish(2)
        for t in range(3):
            taps(0, 2, t)
        relay(3, 2)
        cross(3, 0)
        own_pieces(4, send_piece)
        waits = share_edges(1, lambda s: acc[s], gain2)
        relay(3, 3)
        cross(3, 1)
        relay(3, 4)
        cross(3, 2)
        gather_columns(1, waits)
        clear()
        for k in range(5, 7):
            relay(3, k)
            cross(3, k - 2)
        lax.fori_loop(4, 6, functools.partial(phase_of, phase, 1), 0)
        cross(5, 5)
        cross(5, 6)
        finish(5)
        for t in range(3):
            taps(1, 2, t)
    else:
        gather_columns(0, share_edges(0, read_frame, gain1))
        clear()
        all_taps(0)
        gather_columns(1, share_edges(1, lambda s: acc[s], gain2))
        clear()
        all_taps(1)
    for s in range(slots):
        kept = jnp.where(s < count[0], read_frame(s) + acc[s], 0.0)
        out[s] = kept.astype(BF16).reshape(rows, cols, ch)
    for ok, copy in pending:
        @pl.when(ok)
        def _(copy=copy):
            copy.wait_send()
    if gathers:
        lax.fori_loop(0, 6, drain, 0)


def phase_of(phase, i, n, carry):
    return phase(i, n, carry)


def per_device(
    layout, frames, clip_lengths, group_start, group_count, kernel_one, kernel_two, gain_one, gain_two
):
    nz, ny, nr = layout
    slots, rows, cols, ch = frames.shape
    depth = kernel_one.shape[3]
    gathers = depth % 16 == 0 and (nz, ny, nr) == (4, 2, 4)
    if not gathers:
        kernel_one = lax.all_gather(kernel_one, "group", axis=3, tiled=True)
        kernel_two = lax.all_gather(kernel_two, "group", axis=3, tiled=True)
    vmem = pl.BlockSpec(memory_space=pltpu.VMEM)
    smem = pl.BlockSpec(memory_space=pltpu.SMEM)
    weight_spec = pl.BlockSpec(memory_space=pl.ANY) if gathers else vmem
    full = (6, 3, 3, ch, ch) if gathers else (16, 128)
    shards = lax.axis_size("group")
    dma = pltpu.SemaphoreType.DMA
    return pl.pallas_call(
        functools.partial(kernel, layout, gathers),
        out_shape=jax.ShapeDtypeStruct(frames.shape, BF16),
        in_specs=[vmem, weight_spec, weight_spec, vmem, vmem, smem, smem, smem],
        out_specs=vmem,
        scratch_shapes=[
            pltpu.VMEM(full, BF16),
            pltpu.VMEM((2, slots, rows, cols, ch), BF16),
            pltpu.VMEM((2, 2, rows, cols, ch), BF16),
            pltpu.VMEM((2, slots + 2, rows + 2, cols, ch), BF16),
            pltpu.VMEM((slots + 2, rows + 2, cols, 3 * ch), BF16),
            pltpu.VMEM((slots, rows * cols, ch), F32),
            dma((6, 3, shards) if gathers else (1,)),
            dma((6, shards, 6) if gathers else (1,)),
            dma((2, 5)),
            dma((2, 5)),
            dma((6,)),
        ],
        compiler_params=pltpu.CompilerParams(
            collective_id=0, has_side_effects=True, vmem_limit_bytes=56 * 1024 * 1024
        ),
    )(
        frames, kernel_one, kernel_two, gain_one, gain_two, clip_lengths, group_start, group_count
    )


def solution(mesh):
    groups, rows = mesh.shape["group"], mesh.shape["row"]
    ny = math.isqrt(groups // 2)
    return jax.shard_map(
        functools.partial(per_device, (groups // ny, ny, rows)),
        mesh=mesh,
        in_specs=(
            P("group", "row", None, None),
            P(),
            P("group"),
            P("group"),
            P(None, None, None, "group", None),
            P(None, None, None, "group", None),
            P(),
            P(),
        ),
        out_specs=P("group", "row", None, None),
        check_vma=False,
    )
```

time: 109 us -> 118 us (1.083)
  Pallas kernels: 102 us -> 115 us
  local copies, waits for them, and re-layouts: 4.7 us -> 1.95 us
    pallas_call x1, Pallas kernels: 102 us -> 115 us  [per_device(): pl.pallas_call(functools.partial(kernel, layout, gathers), out_shape=jax....]
    unnamed x9 -> x1, local copies, waits for them, and re-layouts: 2.88 us -> 1.95 us
where the time goes in v2:
time: 118 us
  Pallas kernels  115 us (97%)
  local copies, waits for them, and re-layouts  1.95 us (2%)
  between operations  1.31 us (1%)
    pallas_call x1, Pallas kernels, per_device(): pl.pallas_call(functools.partial(kernel, layout, gathers), out_shape=jax....  115 us

profile of v2, /device:TPU:28, one launch (start us, length us, event | category | flops | bytes accessed | tf_op | source)
XLA Modules:
  0.0 117.9 jit_solution(5240378206551597535)
XLA Ops:
  1.3 114.6 %shard_map.82 = bf16[6,4,32,384]{3,2,1,0:T(8,128)(2,1)} custom-call(bf16[6,4,32,384]{3,2,1,0:T(8,128)(2,1)} %frames.1, bf16[3,3,3,48,384]{4,3,2,1,0:T(8,128)(2,1)} %k1.1, bf16[3,3,3,48,384]{4,3,2,1,0:T(8,128)(2,1)} %k2.1, f32[384]{0:T(512)} %gain1.1, f32[384]{0:T(512)} %gain2.1, s32[3]{0:T(128)} %lengths.1, s32[1]{0:T(128)S(6)} %copy.10.start, s32[1]{0:T(128)S(6)} %copy.11.count), custom_call_target="tpu_custom_call" | custom-call | tf_op jit(solution)/shard_map/pallas_call | solution.py:374
  116.0 2.0 %copy.12 = bf16[6,4,32,384]{3,2,1,0:T(8,128)(2,1)} copy(bf16[6,4,32,384]{3,2,1,0:T(8,128)(2,1)} %shard_map.82) | data formatting | bytes 1179648

commit v3 on v2

--- a/solution.py
+++ b/solution.py
@@ -37,15 +37,14 @@
     pending = []
 
     always = g >= 0
-    up = (z < nz - 1, g + ny, r)
-    down = (z > 0, g - ny, r)
     across = (always, z * ny + (1 - y), r)
     sibling = (always, g, x * 2 + (1 - c))
     other = (always, g, (1 - x) * 2 + (1 - c))
 
     greet = []
     if gathers:
-        greet += [up, down, across, sibling, other]
+        greet += [across, sibling, other]
+        greet += [(always, (z + o) % nz * ny + y, r) for o in range(1, nz)]
     for dr in (-1, 0, 1):
         ok_r = jnp.logical_and(r + dr >= 0, r + dr < nr)
         for dg in (-1, 0, 1):
@@ -98,83 +97,71 @@
                 device_id_type=MESH,
             )
 
-        def send_piece(n, t, s, way, ok, to):
-            @pl.when(ok)
+        def send_piece(n, t, s, way, to):
+            piece_copy(n, t, s, way, to).start()
+
+        def sent_piece(n, t, s, way, to):
+            piece_copy(n, t, s, way, to).wait_send()
+
+        def wait_piece(n, t, s):
+            piece_copy(n, t, s, 0, sibling).wait_recv()
+
+        line = [(z + nz - o) % nz * ny + y for o in range(1, nz)]
+        first = line + [z * ny + (1 - y)]
+        second = [(z + nz - o) % nz * ny + (1 - y) for o in range(1, nz)]
+
+        def own_pieces(n, act_on):
+            for o in range(1, nz):
+                act_on(n, mine, g, o - 1, (always, (z + o) % nz * ny + y, r))
+                if o == 1:
+                    act_on(n, mine, g, 3, across)
+
+        def passed_on(n, group, act_on):
+            for k, s in enumerate(group):
+                if act_on is send_piece:
+                    wait_piece(n, mine, s)
+                if group is first and k < nz - 1:
+                    act_on(n, mine, s, 0, across)
+
+                @pl.when(c == 0)
+                def _(s=s):
+                    act_on(n, mine, s, 1, other)
+                act_on(n, mine, s, 2, sibling)
+
+        def relay(n, group):
+            passed_on(n, group, send_piece)
+
+        def cross(n, group):
+            @pl.when(c == 1)
             def _():
-                piece_copy(n, t, s, way, to).start()
-
-        def sent_piece(n, t, s, way, ok, to):
-            @pl.when(ok)
+                for s in group:
+                    wait_piece(n, 1 - x, s)
+                    send_piece(n, 1 - x, s, 3, sibling)
+
+        def finish(n):
+            for s in first + second:
+                wait_piece(n, 2 * (1 - c) + c * x, s)
+
+            @pl.when(c == 0)
             def _():
-                piece_copy(n, t, s, way, to).wait_send()
-
-        def wait_piece(n, t, s, ok):
-            @pl.when(ok)
-            def _():
-                piece_copy(n, t, s, 0, sibling).wait_recv()
-
-        def both(a, b):
-            return jnp.logical_and(a, b)
-
-        def own_pieces(n, act_on):
-            act_on(n, mine, g, 0, up[0], up)
-            act_on(n, mine, g, 1, down[0], down)
-            act_on(n, mine, g, 2, always, across)
-
-        def arrivals(step):
-            kind, d = step
-            row_y = y if kind == "z" else 1 - y
-            found = []
-            for sign in ((-1, 1) if d else (1,)):
-                zz = z + sign * d
-                ok = both(zz >= 0, zz < nz)
-                s = jnp.clip(zz, 0, nz - 1) * ny + row_y
-                found.append((ok, s, sign))
-            return found
-
-        steps = [("z", 1), ("y", 0)]
-        for d in range(2, nz):
-            steps += [("z", d), ("y", d - 1)]
-        steps += [("y", nz - 1)]
-
-        def passed_on(n, step, ok, s, sign, act_on):
-            if step[0] == "z":
-                if sign < 0:
-                    act_on(n, mine, s, 0, both(ok, up[0]), up)
-                else:
-                    act_on(n, mine, s, 1, both(ok, down[0]), down)
-                act_on(n, mine, s, 2, ok, across)
-            act_on(n, mine, s, 3, both(ok, c == 0), other)
-            act_on(n, mine, s, 4, ok, sibling)
-
-        def relay(n, k):
-            for ok, s, sign in arrivals(steps[k]):
-                wait_piece(n, mine, s, ok)
-                passed_on(n, steps[k], ok, s, sign, send_piece)
-
-        def cross(n, k):
-            for ok, s, _ in arrivals(steps[k]):
-                here = both(ok, c == 1)
-                wait_piece(n, 1 - x, s, here)
-                send_piece(n, 1 - x, s, 5, here, sibling)
-
-        def finish(n):
-            for step in steps:
-                for ok, s, _ in arrivals(step):
-                    wait_piece(n, 2 * (1 - c) + c * x, s, ok)
-                    wait_piece(n, 1 - x, s, both(ok, c == 0))
+                for s in first + second:
+                    wait_piece(n, 1 - x, s)
 
         def drain(n, carry):
             own_pieces(n, sent_piece)
-            for step in steps:
-                for ok, s, sign in arrivals(step):
-                    passed_on(n, step, ok, s, sign, sent_piece)
-                    sent_piece(n, 1 - x, s, 5, both(ok, c == 1), sibling)
+            passed_on(n, first, sent_piece)
+            passed_on(n, second, sent_piece)
+
+            @pl.when(c == 1)
+            def _():
+                for s in first + second:
+                    sent_piece(n, 1 - x, s, 3, sibling)
             return carry
 
         for landing in landings:
             landing.wait()
         own_pieces(0, send_piece)
+        own_pieces(1, send_piece)
 
     def share_edges(i, read, gain):
         for s in range(slots):
@@ -264,26 +251,18 @@
     def read_frame(s):
         return frames[s].reshape(per, ch).astype(F32)
 
-    def phase(i, n, carry=0):
-        relay(n, 0)
-        cross(n - 1, 5)
-        relay(n, 1)
-        cross(n - 1, 6)
+    def phase(i, n, carry):
+        relay(n, first)
+        cross(n - 1, second)
+
+        @pl.when(n < 4)
+        def _():
+            own_pieces(n + 2, send_piece)
         finish(n - 1)
-        taps(i, n - 1 - 3 * i, 0)
-        relay(n, 2)
-        cross(n, 0)
-
-        @pl.when(n < 5)
-        def _():
-            own_pieces(n + 1, send_piece)
-        taps(i, n - 1 - 3 * i, 1)
-        relay(n, 3)
-        cross(n, 1)
-        taps(i, n - 1 - 3 * i, 2)
-        for k in range(4, 7):
-            relay(n, k)
-            cross(n, k - 2)
+        for t in range(3):
+            taps(i, n - 1 - 3 * i, t)
+        relay(n, second)
+        cross(n, first)
         return carry
 
     def all_taps(i):
@@ -296,40 +275,26 @@
 
     if gathers:
         waits = share_edges(0, read_frame, gain1)
-        relay(0, 0)
-        relay(0, 1)
+        relay(0, first)
+        own_pieces(2, send_piece)
         gather_columns(0, waits)
         clear()
-        relay(0, 2)
-        cross(0, 0)
-        own_pieces(1, send_piece)
-        for k in range(3, 7):
-            relay(0, k)
-            cross(0, k - 2)
-        lax.fori_loop(1, 3, functools.partial(phase_of, phase, 0), 0)
-        relay(3, 0)
-        cross(2, 5)
-        relay(3, 1)
-        cross(2, 6)
+        relay(0, second)
+        cross(0, first)
+        lax.fori_loop(1, 3, functools.partial(phase, 0), 0)
+        relay(3, first)
+        cross(2, second)
+        own_pieces(5, send_piece)
         finish(2)
         for t in range(3):
             taps(0, 2, t)
-        relay(3, 2)
-        cross(3, 0)
-        own_pieces(4, send_piece)
         waits = share_edges(1, lambda s: acc[s], gain2)
-        relay(3, 3)
-        cross(3, 1)
-        relay(3, 4)
-        cross(3, 2)
+        relay(3, second)
+        cross(3, first)
         gather_columns(1, waits)
         clear()
-        for k in range(5, 7):
-            relay(3, k)
-            cross(3, k - 2)
-        lax.fori_loop(4, 6, functools.partial(phase_of, phase, 1), 0)
-        cross(5, 5)
-        cross(5, 6)
+        lax.fori_loop(4, 6, functools.partial(phase, 1), 0)
+        cross(5, second)
         finish(5)
         for t in range(3):
             taps(1, 2, t)
@@ -349,10 +314,6 @@
             copy.wait_send()
     if gathers:
         lax.fori_loop(0, 6, drain, 0)
-
-
-def phase_of(phase, i, n, carry):
-    return phase(i, n, carry)
 
 
 def per_device(
@@ -384,7 +345,7 @@
             pltpu.VMEM((slots + 2, rows + 2, cols, 3 * ch), BF16),
             pltpu.VMEM((slots, rows * cols, ch), F32),
             dma((6, 3, shards) if gathers else (1,)),
-            dma((6, shards, 6) if gathers else (1,)),
+            dma((6, shards, 4) if gathers else (1,)),
             dma((2, 5)),
             dma((2, 5)),
             dma((6,)),

time: 118 us -> 112 us (0.949)
  the two profiles are of different devices: /device:TPU:28 before, /device:TPU:18 now
where the time goes in v3:
time: 112 us
  Pallas kernels  109 us (97%)
  local copies, waits for them, and re-layouts  1.95 us (2%)
  between operations  1.3 us (1%)
    pallas_call x1, Pallas kernels, per_device(): pl.pallas_call(functools.partial(kernel, layout, gathers), out_shape=jax....  109 us

profile of v3, /device:TPU:18, one launch (start us, length us, event | category | flops | bytes accessed | tf_op | source)
XLA Modules:
  0.0 112.1 jit_solution(6035804139820966449)
XLA Ops:
  1.3 108.8 %shard_map.82 = bf16[6,4,32,384]{3,2,1,0:T(8,128)(2,1)} custom-call(bf16[6,4,32,384]{3,2,1,0:T(8,128)(2,1)} %frames.1, bf16[3,3,3,48,384]{4,3,2,1,0:T(8,128)(2,1)} %k1.1, bf16[3,3,3,48,384]{4,3,2,1,0:T(8,128)(2,1)} %k2.1, f32[384]{0:T(512)} %gain1.1, f32[384]{0:T(512)} %gain2.1, s32[3]{0:T(128)} %lengths.1, s32[1]{0:T(128)S(6)} %copy.10.start, s32[1]{0:T(128)S(6)} %copy.11.count), custom_call_target="tpu_custom_call" | custom-call | tf_op jit(solution)/shard_map/pallas_call | solution.py:335
  110.1 2.0 %copy.12 = bf16[6,4,32,384]{3,2,1,0:T(8,128)(2,1)} copy(bf16[6,4,32,384]{3,2,1,0:T(8,128)(2,1)} %shard_map.82) | data formatting | bytes 1179648

commit v4 on v3

--- a/solution.py
+++ b/solution.py
@@ -53,11 +53,10 @@
             ok = jnp.logical_and(ok_r, jnp.logical_and(g + dg >= 0, g + dg < ng))
             greet.append((ok, g + dg, r + dr))
     if gathers:
-        depth = k1.shape[3]
-        own = pl.ds(pl.multiple_of(g * depth, depth), depth)
+        mine = 2 * c + (1 - c) * x
         landings = [
             pltpu.make_async_copy(
-                kernels[n // 3].at[:, n % 3], w.at[n, :, :, own, :], own_sem.at[n]
+                kernels[n // 3].at[mine, n % 3], w.at[n, mine, :, z, y], own_sem.at[n]
             )
             for n in range(6)
         ]
@@ -84,84 +83,92 @@
         pending.append((ok, copy))
 
     if gathers:
-        mine = 2 * c + (1 - c) * x
-
-        def piece(n, t, s):
-            return w.at[n, t, :, pl.ds(pl.multiple_of(s * depth, depth), depth), :]
-
-        def piece_copy(n, t, s, way, to):
-            there = piece(n, t, s)
+        def copy_of(n, sem, there, to):
             return pltpu.make_async_remote_copy(
-                src_ref=there, dst_ref=there, send_sem=piece_send.at[n, s, way],
-                recv_sem=piece_recv.at[n, t, s], device_id=(to[1], to[2]),
+                src_ref=there, dst_ref=there, send_sem=piece_send.at[n, sem],
+                recv_sem=piece_recv.at[n, sem], device_id=(to[1], to[2]),
                 device_id_type=MESH,
             )
 
-        def send_piece(n, t, s, way, to):
-            piece_copy(n, t, s, way, to).start()
-
-        def sent_piece(n, t, s, way, to):
-            piece_copy(n, t, s, way, to).wait_send()
-
-        def wait_piece(n, t, s):
-            piece_copy(n, t, s, 0, sibling).wait_recv()
-
-        line = [(z + nz - o) % nz * ny + y for o in range(1, nz)]
-        first = line + [z * ny + (1 - y)]
-        second = [(z + nz - o) % nz * ny + (1 - y) for o in range(1, nz)]
-
-        def own_pieces(n, act_on):
+        def line(n, t, row_y):
+            return w.at[n, t, :, :, row_y]
+
+        def along(n, o):
+            to = (always, (z + o) % nz * ny + y, r)
+            return copy_of(n, o - 1, w.at[n, mine, :, z, y], to)
+
+        def came_along(n, o):
+            there = w.at[n, mine, :, (z + nz - o) % nz, y]
+            return copy_of(n, o - 1, there, sibling)
+
+        ys = (y, 1 - y)
+
+        def over_y(n):
+            return copy_of(n, 3, line(n, mine, y), across)
+
+        def over_x(n, k):
+            return copy_of(n, 4 + k, line(n, mine, ys[k]), other)
+
+        def to_sibling(n, k):
+            return copy_of(n, 6 + k, line(n, mine, ys[k]), sibling)
+
+        def crossed(n, k):
+            return copy_of(n, 8 + k, line(n, 1 - x, ys[k]), sibling)
+
+        def own_pieces(n):
             for o in range(1, nz):
-                act_on(n, mine, g, o - 1, (always, (z + o) % nz * ny + y, r))
-                if o == 1:
-                    act_on(n, mine, g, 3, across)
-
-        def passed_on(n, group, act_on):
-            for k, s in enumerate(group):
-                if act_on is send_piece:
-                    wait_piece(n, mine, s)
-                if group is first and k < nz - 1:
-                    act_on(n, mine, s, 0, across)
-
-                @pl.when(c == 0)
-                def _(s=s):
-                    act_on(n, mine, s, 1, other)
-                act_on(n, mine, s, 2, sibling)
-
-        def relay(n, group):
-            passed_on(n, group, send_piece)
-
-        def cross(n, group):
+                along(n, o).start()
+
+        def share(n, k):
+            @pl.when(c == 0)
+            def _():
+                over_x(n, k).start()
+            to_sibling(n, k).start()
+
+        def first(n):
+            for o in range(1, nz):
+                came_along(n, o).wait_recv()
+            over_y(n).start()
+            share(n, 0)
+
+        def second(n):
+            copy_of(n, 3, line(n, mine, 1 - y), sibling).wait_recv()
+            share(n, 1)
+
+        def cross(n, k):
             @pl.when(c == 1)
             def _():
-                for s in group:
-                    wait_piece(n, 1 - x, s)
-                    send_piece(n, 1 - x, s, 3, sibling)
+                copy_of(n, 4 + k, line(n, 1 - x, ys[k]), sibling).wait_recv()
+                crossed(n, k).start()
 
         def finish(n):
-            for s in first + second:
-                wait_piece(n, 2 * (1 - c) + c * x, s)
-
-            @pl.when(c == 0)
-            def _():
-                for s in first + second:
-                    wait_piece(n, 1 - x, s)
+            for k in range(2):
+                copy_of(n, 6 + k, line(n, 2 * (1 - c) + c * x, ys[k]), sibling).wait_recv()
+
+                @pl.when(c == 0)
+                def _(k=k):
+                    crossed(n, k).wait_recv()
 
         def drain(n, carry):
-            own_pieces(n, sent_piece)
-            passed_on(n, first, sent_piece)
-            passed_on(n, second, sent_piece)
-
-            @pl.when(c == 1)
-            def _():
-                for s in first + second:
-                    sent_piece(n, 1 - x, s, 3, sibling)
+            for o in range(1, nz):
+                along(n, o).wait_send()
+            over_y(n).wait_send()
+            for k in range(2):
+                to_sibling(n, k).wait_send()
+
+                @pl.when(c == 0)
+                def _(k=k):
+                    over_x(n, k).wait_send()
+
+                @pl.when(c == 1)
+                def _(k=k):
+                    crossed(n, k).wait_send()
             return carry
 
         for landing in landings:
             landing.wait()
-        own_pieces(0, send_piece)
-        own_pieces(1, send_piece)
+        own_pieces(0)
+        own_pieces(1)
 
     def share_edges(i, read, gain):
         for s in range(slots):
@@ -238,73 +245,47 @@
             begin = jnp.where(end <= frame, jnp.maximum(begin, end), begin)
         position.append(frame - begin)
 
-    def taps(i, p, t):
-        lhs = a3[t : t + slots, pl.ds(p, rows)].reshape(slots * per, 3 * ch)
-        held = w[3 * i + p, t] if gathers else kernels[i][t, p]
-        part = jnp.dot(lhs, held.reshape(3 * ch, ch), preferred_element_type=F32)
-        for s in range(slots):
-            here = part[s * per : (s + 1) * per]
-            if t < 2:
-                here = here * jnp.where(position[s] >= 2 - t, 1.0, 0.0)
-            acc[s] += here
+    def taps(i, p):
+        def body(t, carry):
+            lhs = a3[pl.ds(t, slots), p : p + rows].reshape(slots * per, 3 * ch)
+            held = w[3 * i + p, t] if gathers else kernels[i][t, p]
+            part = jnp.dot(lhs, held.reshape(3 * ch, ch), preferred_element_type=F32)
+            for s in range(slots):
+                kept = jnp.where(position[s] >= 2 - t, 1.0, 0.0)
+                acc[s] += part[s * per : (s + 1) * per] * kept
+            return carry
+
+        lax.fori_loop(0, 3, body, 0)
 
     def read_frame(s):
         return frames[s].reshape(per, ch).astype(F32)
 
-    def phase(i, n, carry):
-        relay(n, first)
-        cross(n - 1, second)
-
-        @pl.when(n < 4)
-        def _():
-            own_pieces(n + 2, send_piece)
-        finish(n - 1)
-        for t in range(3):
-            taps(i, n - 1 - 3 * i, t)
-        relay(n, second)
-        cross(n, first)
-        return carry
-
-    def all_taps(i):
-        def body(p, carry):
-            for t in range(3):
-                taps(i, p, t)
-            return carry
-
-        lax.fori_loop(0, 3, body, 0)
-
-    if gathers:
-        waits = share_edges(0, read_frame, gain1)
-        relay(0, first)
-        own_pieces(2, send_piece)
-        gather_columns(0, waits)
-        clear()
-        relay(0, second)
-        cross(0, first)
-        lax.fori_loop(1, 3, functools.partial(phase, 0), 0)
-        relay(3, first)
-        cross(2, second)
-        own_pieces(5, send_piece)
-        finish(2)
-        for t in range(3):
-            taps(0, 2, t)
-        waits = share_edges(1, lambda s: acc[s], gain2)
-        relay(3, second)
-        cross(3, first)
-        gather_columns(1, waits)
-        clear()
-        lax.fori_loop(4, 6, functools.partial(phase, 1), 0)
-        cross(5, second)
-        finish(5)
-        for t in range(3):
-            taps(1, 2, t)
-    else:
-        gather_columns(0, share_edges(0, read_frame, gain1))
-        clear()
-        all_taps(0)
-        gather_columns(1, share_edges(1, lambda s: acc[s], gain2))
-        clear()
-        all_taps(1)
+    for n in range(8):
+        if gathers:
+            if n == 0:
+                waits = share_edges(0, read_frame, gain1)
+            if n < 6:
+                first(n)
+            if n + 2 < 6:
+                own_pieces(n + 2)
+            if 0 <= n - 1 < 6:
+                second(n - 1)
+                cross(n - 1, 0)
+            if n >= 2:
+                cross(n - 2, 1)
+                finish(n - 2)
+        elif n == 0:
+            waits = share_edges(0, read_frame, gain1)
+        if n == 0:
+            gather_columns(0, waits)
+            clear()
+        if n == 5:
+            gather_columns(1, waits)
+            clear()
+        if n >= 2:
+            taps((n - 2) // 3, (n - 2) % 3)
+        if n == 4:
+            waits = share_edges(1, lambda s: acc[s], gain2)
     for s in range(slots):
         kept = jnp.where(s < count[0], read_frame(s) + acc[s], 0.0)
         out[s] = kept.astype(BF16).reshape(rows, cols, ch)
@@ -329,8 +310,7 @@
     vmem = pl.BlockSpec(memory_space=pltpu.VMEM)
     smem = pl.BlockSpec(memory_space=pltpu.SMEM)
     weight_spec = pl.BlockSpec(memory_space=pl.ANY) if gathers else vmem
-    full = (6, 3, 3, ch, ch) if gathers else (16, 128)
-    shards = lax.axis_size("group")
+    full = (6, 3, 3, nz, ny, depth, ch) if gathers else (16, 128)
     dma = pltpu.SemaphoreType.DMA
     return pl.pallas_call(
         functools.partial(kernel, layout, gathers),
@@ -344,8 +324,8 @@
             pltpu.VMEM((2, slots + 2, rows + 2, cols, ch), BF16),
             pltpu.VMEM((slots + 2, rows + 2, cols, 3 * ch), BF16),
             pltpu.VMEM((slots, rows * cols, ch), F32),
-            dma((6, 3, shards) if gathers else (1,)),
-            dma((6, shards, 4) if gathers else (1,)),
+            dma((6, 10) if gathers else (1,)),
+            dma((6, 10) if gathers else (1,)),
             dma((2, 5)),
             dma((2, 5)),
             dma((6,)),

time: 112 us -> 115 us (1.027)
  the two profiles are of different devices: /device:TPU:18 before, /device:TPU:26 now
where the time goes in v4:
time: 115 us
  Pallas kernels  112 us (97%)
  local copies, waits for them, and re-layouts  1.95 us (2%)
  between operations  1.3 us (1%)
    pallas_call x1, Pallas kernels, per_device(): pl.pallas_call(functools.partial(kernel, layout, gathers), out_shape=jax....  112 us

profile of v4, /device:TPU:26, one launch (start us, length us, event | category | flops | bytes accessed | tf_op | source)
XLA Modules:
  0.0 114.8 jit_solution(4807538025975966342)
XLA Ops:
  1.3 111.5 %shard_map.82 = bf16[6,4,32,384]{3,2,1,0:T(8,128)(2,1)} custom-call(bf16[6,4,32,384]{3,2,1,0:T(8,128)(2,1)} %frames.1, bf16[3,3,3,48,384]{4,3,2,1,0:T(8,128)(2,1)} %k1.1, bf16[3,3,3,48,384]{4,3,2,1,0:T(8,128)(2,1)} %k2.1, f32[384]{0:T(512)} %gain1.1, f32[384]{0:T(512)} %gain2.1, s32[3]{0:T(128)} %lengths.1, s32[1]{0:T(128)S(6)} %copy.10.start, s32[1]{0:T(128)S(6)} %copy.11.count), custom_call_target="tpu_custom_call" | custom-call | tf_op jit(solution)/shard_map/pallas_call | solution.py:315
  112.8 2.0 %copy.12 = bf16[6,4,32,384]{3,2,1,0:T(8,128)(2,1)} copy(bf16[6,4,32,384]{3,2,1,0:T(8,128)(2,1)} %shard_map.82) | data formatting | bytes 1179648

commit v5 on v3

--- a/solution.py
+++ b/solution.py
@@ -43,7 +43,7 @@
 
     greet = []
     if gathers:
-        greet += [across, sibling, other]
+        greet += [across, sibling, other, (always, g, (1 - x) * 2 + c)]
         greet += [(always, (z + o) % nz * ny + y, r) for o in range(1, nz)]
     for dr in (-1, 0, 1):
         ok_r = jnp.logical_and(r + dr >= 0, r + dr < nr)
@@ -106,22 +106,45 @@
         def wait_piece(n, t, s):
             piece_copy(n, t, s, 0, sibling).wait_recv()
 
-        line = [(z + nz - o) % nz * ny + y for o in range(1, nz)]
+        gaps = [jnp.where(z < 2, nz - o, o) for o in range(1, nz)]
+        line = [(z + nz - gap) % nz * ny + y for gap in gaps]
+        inner = jnp.logical_and(z > 0, z < nz - 1)
+        far_end = (always, (nz - 1) * (z - 1) * ny + y, r)
+        level = (always, g, (1 - x) * 2 + c)
         first = line + [z * ny + (1 - y)]
-        second = [(z + nz - o) % nz * ny + (1 - y) for o in range(1, nz)]
+        second = [(z + nz - gap) % nz * ny + (1 - y) for gap in gaps]
 
         def own_pieces(n, act_on):
             for o in range(1, nz):
-                act_on(n, mine, g, o - 1, (always, (z + o) % nz * ny + y, r))
+                zz = (z + o) % nz
+
+                @pl.when(jnp.abs(zz - z) < nz - 1)
+                def _(o=o, zz=zz):
+                    act_on(n, mine, g, o - 1, (always, zz * ny + y, r))
                 if o == 1:
                     act_on(n, mine, g, 3, across)
+
+        def in_turn(n):
+            return (n + x) % 2 == 0
 
         def passed_on(n, group, act_on):
             for k, s in enumerate(group):
                 if act_on is send_piece:
                     wait_piece(n, mine, s)
-                if group is first and k < nz - 1:
+                if group is first and k == 1:
+                    @pl.when(inner)
+                    def _(s=s):
+                        act_on(n, mine, s, 4, far_end)
+
+                    @pl.when(jnp.logical_or(c == 0, in_turn(n)))
+                    def _(s=s):
+                        act_on(n, mine, s, 0, across)
+                elif group is first and k < nz - 1:
                     act_on(n, mine, s, 0, across)
+                if group is second and k == 1:
+                    @pl.when(jnp.logical_and(c == 1, in_turn(n)))
+                    def _(s=s):
+                        act_on(n, mine, s, 4, level)
 
                 @pl.when(c == 0)
                 def _(s=s):
@@ -345,7 +368,7 @@
             pltpu.VMEM((slots + 2, rows + 2, cols, 3 * ch), BF16),
             pltpu.VMEM((slots, rows * cols, ch), F32),
             dma((6, 3, shards) if gathers else (1,)),
-            dma((6, shards, 4) if gathers else (1,)),
+            dma((6, shards, 5) if gathers else (1,)),
             dma((2, 5)),
             dma((2, 5)),
             dma((6,)),

time: 112 us -> 108 us (0.964)
  the two profiles are of different devices: /device:TPU:18 before, /device:TPU:0 now
where the time goes in v5:
time: 108 us; the launch traced here: 107 us
  Pallas kernels  104 us (96%)
  local copies, waits for them, and re-layouts  1.95 us (2%)
  between operations  1.31 us (1%)
    pallas_call x1, Pallas kernels, per_device(): pl.pallas_call(functools.partial(kernel, layout, gathers), out_shape=jax....  104 us

profile of v5, /device:TPU:0, one launch (start us, length us, event | category | flops | bytes accessed | tf_op | source)
XLA Modules:
  0.0 107.5 jit_solution(1759032511079554302)
XLA Ops:
  1.3 104.2 %shard_map.82 = bf16[6,4,32,384]{3,2,1,0:T(8,128)(2,1)} custom-call(bf16[6,4,32,384]{3,2,1,0:T(8,128)(2,1)} %frames.1, bf16[3,3,3,48,384]{4,3,2,1,0:T(8,128)(2,1)} %k1.1, bf16[3,3,3,48,384]{4,3,2,1,0:T(8,128)(2,1)} %k2.1, f32[384]{0:T(512)} %gain1.1, f32[384]{0:T(512)} %gain2.1, s32[3]{0:T(128)} %lengths.1, s32[1]{0:T(128)S(6)} %copy.10.start, s32[1]{0:T(128)S(6)} %copy.11.count), custom_call_target="tpu_custom_call" | custom-call | tf_op jit(solution)/shard_map/pallas_call | solution.py:358
  105.5 2.0 %copy.12 = bf16[6,4,32,384]{3,2,1,0:T(8,128)(2,1)} copy(bf16[6,4,32,384]{3,2,1,0:T(8,128)(2,1)} %shard_map.82) | data formatting | bytes 1179648

commit v6 on v5

--- a/solution.py
+++ b/solution.py
@@ -261,71 +261,76 @@
             begin = jnp.where(end <= frame, jnp.maximum(begin, end), begin)
         position.append(frame - begin)
 
-    def taps(i, p, t):
-        lhs = a3[t : t + slots, pl.ds(p, rows)].reshape(slots * per, 3 * ch)
-        held = w[3 * i + p, t] if gathers else kernels[i][t, p]
-        part = jnp.dot(lhs, held.reshape(3 * ch, ch), preferred_element_type=F32)
-        for s in range(slots):
-            here = part[s * per : (s + 1) * per]
-            if t < 2:
-                here = here * jnp.where(position[s] >= 2 - t, 1.0, 0.0)
-            acc[s] += here
+    def taps(i, p):
+        def body(t, carry):
+            lhs = a3[pl.ds(t, slots), pl.ds(p, rows)].reshape(slots * per, 3 * ch)
+            held = w[3 * i + p, t] if gathers else kernels[i][t, p]
+            part = jnp.dot(lhs, held.reshape(3 * ch, ch), preferred_element_type=F32)
+            for s in range(slots):
+                kept = jnp.where(position[s] >= 2 - t, 1.0, 0.0)
+                acc[s] += part[s * per : (s + 1) * per] * kept
+            return carry
+
+        lax.fori_loop(0, 3, body, 0)
 
     def read_frame(s):
         return frames[s].reshape(per, ch).astype(F32)
 
-    def phase(i, n, carry):
+    def tick(n, more):
         relay(n, first)
-        cross(n - 1, second)
-
-        @pl.when(n < 4)
-        def _():
+        if more:
             own_pieces(n + 2, send_piece)
-        finish(n - 1)
-        for t in range(3):
-            taps(i, n - 1 - 3 * i, t)
-        relay(n, second)
-        cross(n, first)
+        relay(n - 1, second)
+        cross(n - 1, first)
+        cross(n - 2, second)
+        finish(n - 2)
+
+    def early(n, carry):
+        tick(n, True)
+        taps(0, n - 2)
         return carry
 
     def all_taps(i):
         def body(p, carry):
-            for t in range(3):
-                taps(i, p, t)
+            taps(i, p)
             return carry
 
         lax.fori_loop(0, 3, body, 0)
 
+    def edges_again():
+        return share_edges(1, lambda s: acc[s], gain2)
+
+    waits = share_edges(0, read_frame, gain1)
     if gathers:
-        waits = share_edges(0, read_frame, gain1)
         relay(0, first)
         own_pieces(2, send_piece)
         gather_columns(0, waits)
         clear()
+        relay(1, first)
+        own_pieces(3, send_piece)
         relay(0, second)
         cross(0, first)
-        lax.fori_loop(1, 3, functools.partial(phase, 0), 0)
-        relay(3, first)
-        cross(2, second)
-        own_pieces(5, send_piece)
-        finish(2)
-        for t in range(3):
-            taps(0, 2, t)
-        waits = share_edges(1, lambda s: acc[s], gain2)
-        relay(3, second)
-        cross(3, first)
+        lax.fori_loop(2, 4, early, 0)
+        tick(4, False)
+        taps(0, 2)
+        waits = edges_again()
+        tick(5, False)
         gather_columns(1, waits)
         clear()
-        lax.fori_loop(4, 6, functools.partial(phase, 1), 0)
+        taps(1, 0)
+        relay(5, second)
+        cross(5, first)
+        cross(4, second)
+        finish(4)
+        taps(1, 1)
         cross(5, second)
         finish(5)
-        for t in range(3):
-            taps(1, 2, t)
+        taps(1, 2)
     else:
-        gather_columns(0, share_edges(0, read_frame, gain1))
+        gather_columns(0, waits)
         clear()
         all_taps(0)
-        gather_columns(1, share_edges(1, lambda s: acc[s], gain2))
+        gather_columns(1, edges_again())
         clear()
         all_taps(1)
     for s in range(slots):

time: 108 us -> 99.9 us (0.925)
  the two profiles are of different devices: /device:TPU:0 before, /device:TPU:28 now
where the time goes in v6:
time: 99.9 us; the launch traced here: 99.7 us
  Pallas kernels  96.5 us (97%)
  local copies, waits for them, and re-layouts  1.95 us (2%)
  between operations  1.3 us (1%)
    pallas_call x1, Pallas kernels, per_device(): pl.pallas_call(functools.partial(kernel, layout, gathers), out_shape=jax....  96.5 us

profile of v6, /device:TPU:28, one launch (start us, length us, event | category | flops | bytes accessed | tf_op | source)
XLA Modules:
  0.0 99.7 jit_solution(15711754033959960183)
XLA Ops:
  1.3 96.5 %shard_map.82 = bf16[6,4,32,384]{3,2,1,0:T(8,128)(2,1)} custom-call(bf16[6,4,32,384]{3,2,1,0:T(8,128)(2,1)} %frames.1, bf16[3,3,3,48,384]{4,3,2,1,0:T(8,128)(2,1)} %k1.1, bf16[3,3,3,48,384]{4,3,2,1,0:T(8,128)(2,1)} %k2.1, f32[384]{0:T(512)} %gain1.1, f32[384]{0:T(512)} %gain2.1, s32[3]{0:T(128)} %lengths.1, s32[1]{0:T(128)S(6)} %copy.10.start, s32[1]{0:T(128)S(6)} %copy.11.count), custom_call_target="tpu_custom_call" | custom-call | tf_op jit(solution)/shard_map/pallas_call | solution.py:363
  97.8 2.0 %copy.12 = bf16[6,4,32,384]{3,2,1,0:T(8,128)(2,1)} copy(bf16[6,4,32,384]{3,2,1,0:T(8,128)(2,1)} %shard_map.82) | data formatting | bytes 1179648

commit v7 on v6

--- a/solution.py
+++ b/solution.py
@@ -43,7 +43,7 @@
 
     greet = []
     if gathers:
-        greet += [across, sibling, other, (always, g, (1 - x) * 2 + c)]
+        greet += [across, sibling, other]
         greet += [(always, (z + o) % nz * ny + y, r) for o in range(1, nz)]
     for dr in (-1, 0, 1):
         ok_r = jnp.logical_and(r + dr >= 0, r + dr < nr)
@@ -110,7 +110,6 @@
         line = [(z + nz - gap) % nz * ny + y for gap in gaps]
         inner = jnp.logical_and(z > 0, z < nz - 1)
         far_end = (always, (nz - 1) * (z - 1) * ny + y, r)
-        level = (always, g, (1 - x) * 2 + c)
         first = line + [z * ny + (1 - y)]
         second = [(z + nz - gap) % nz * ny + (1 - y) for gap in gaps]
 
@@ -123,9 +122,6 @@
                     act_on(n, mine, g, o - 1, (always, zz * ny + y, r))
                 if o == 1:
                     act_on(n, mine, g, 3, across)
-
-        def in_turn(n):
-            return (n + x) % 2 == 0
 
         def passed_on(n, group, act_on):
             for k, s in enumerate(group):
@@ -135,16 +131,20 @@
                     @pl.when(inner)
                     def _(s=s):
                         act_on(n, mine, s, 4, far_end)
-
-                    @pl.when(jnp.logical_or(c == 0, in_turn(n)))
+                if group is first and k < nz - 1:
+                    far = k == 1 if k < 2 else jnp.logical_not(inner)
+
+                    @pl.when(jnp.logical_or(c == 0, far))
                     def _(s=s):
                         act_on(n, mine, s, 0, across)
-                elif group is first and k < nz - 1:
-                    act_on(n, mine, s, 0, across)
-                if group is second and k == 1:
-                    @pl.when(jnp.logical_and(c == 1, in_turn(n)))
+                elif group is first:
+                    @pl.when(jnp.logical_and(c == 1, z < nz - 1))
                     def _(s=s):
-                        act_on(n, mine, s, 4, level)
+                        act_on(n, mine, s, 5, (always, g + ny, r))
+
+                    @pl.when(jnp.logical_and(c == 1, z > 0))
+                    def _(s=s):
+                        act_on(n, mine, s, 6, (always, g - ny, r))
 
                 @pl.when(c == 0)
                 def _(s=s):
@@ -373,7 +373,7 @@
             pltpu.VMEM((slots + 2, rows + 2, cols, 3 * ch), BF16),
             pltpu.VMEM((slots, rows * cols, ch), F32),
             dma((6, 3, shards) if gathers else (1,)),
-            dma((6, shards, 5) if gathers else (1,)),
+            dma((6, shards, 7) if gathers else (1,)),
             dma((2, 5)),
             dma((2, 5)),
             dma((6,)),

time: 99.9 us -> 97.1 us (0.972)
  Pallas kernels: 96.5 us -> 93.7 us
    pallas_call x1, Pallas kernels: 96.5 us -> 93.7 us  [per_device(): pl.pallas_call(functools.partial(kernel, layout, gathers), out_shape=jax....]
where the time goes in v7:
time: 97.1 us; the launch traced here: 96.9 us
  Pallas kernels  93.7 us (96%)
  local copies, waits for them, and re-layouts  1.95 us (2%)
  between operations  1.3 us (1%)
    pallas_call x1, Pallas kernels, per_device(): pl.pallas_call(functools.partial(kernel, layout, gathers), out_shape=jax....  93.7 us
    unnamed x1, local copies, waits for them, and re-layouts  1.95 us

profile of v7, /device:TPU:28, one launch (start us, length us, event | category | flops | bytes accessed | tf_op | source)
XLA Modules:
  0.0 96.9 jit_solution(12351772477015101617)
XLA Ops:
  1.3 93.7 %shard_map.82 = bf16[6,4,32,384]{3,2,1,0:T(8,128)(2,1)} custom-call(bf16[6,4,32,384]{3,2,1,0:T(8,128)(2,1)} %frames.1, bf16[3,3,3,48,384]{4,3,2,1,0:T(8,128)(2,1)} %k1.1, bf16[3,3,3,48,384]{4,3,2,1,0:T(8,128)(2,1)} %k2.1, f32[384]{0:T(512)} %gain1.1, f32[384]{0:T(512)} %gain2.1, s32[3]{0:T(128)} %lengths.1, s32[1]{0:T(128)S(6)} %copy.10.start, s32[1]{0:T(128)S(6)} %copy.11.count), custom_call_target="tpu_custom_call" | custom-call | tf_op jit(solution)/shard_map/pallas_call | solution.py:363
  95.0 2.0 %copy.12 = bf16[6,4,32,384]{3,2,1,0:T(8,128)(2,1)} copy(bf16[6,4,32,384]{3,2,1,0:T(8,128)(2,1)} %shard_map.82) | data formatting | bytes 1179648
